TPU v7x, 256 devices: a whole 4x4x8 slice. The times are simulated.
256 devices in a mesh: row: 16 (over z, x_hi), col: 16 (over x_lo, y, core).
Axes of the slice: x: 4 (x_hi: 2, x_lo: 2; x = x_hi * 2 + x_lo), y: 4, z: 8, core: 2. Of those that a mesh axis runs over, the one named last changes fastest.
Arguments:
- inverse: float32 [24576, 24576], P('row', 'col'), may hold values from -0.15625 to 0.15625
- pattern: int32 [48, 48], replicated, may hold values from 0 to 1, as said below
- factor: float32 [24576, 1024], P(('row', 'col')), may hold values from -0.3125 to 0.3125
- diag_inverse: float32 [1024, 1024], replicated, may hold values from -6 to 6
Outputs:
- panel_out: float32 [24576, 1024], P(('row', 'col'))
- diag_block: float32 [1024, 1024], replicated
Inputs may be any that keep to these rules, and one draw needn't show every extreme that they name: pattern[i, j] is 1 where tile (i, j) of the inverse is stored, else 0.
All inputs are finite; a program needn't handle non-finite values.
Results may differ from a plain program's by a relative error of at most 0.000075.
Values sent between devices are 32-bit elements; how exact they have to be, the bound alone decides.
A program may use at most 128 MiB of HBM per device.

v0:
```python
import jax
import jax.numpy as jnp
from jax import lax
from jax.sharding import Mesh
from jax.sharding import PartitionSpec as P

B = 512
W = 1024
ROW = ("row_0", "row_1")
ROW_COL = ("row_0", "row_1", "col")


HIGHEST = lax.Precision.HIGHEST


def gather_axes(value, axes, dim):
    if not axes:
        return value
    nearer = lax.all_gather(value, axes[-1], axis=dim, tiled=True)
    return gather_axes(nearer, axes[:-1], dim)


def add_product(running, tile_row, inv_block, rows_part):
    first = tile_row * B
    current = lax.dynamic_slice_in_dim(running, first, B, 0)
    update = current + jnp.dot(inv_block, rows_part, precision=HIGHEST)
    return lax.dynamic_update_slice_in_dim(running, update, first, 0)


def stored_list(pattern, first_row, first_col, tile_rows, tile_cols):
    window = lax.dynamic_slice(pattern, (first_row, first_col), (tile_rows, tile_cols)).reshape(-1)
    count_all = tile_rows * tile_cols
    places = jnp.where(window > 0, jnp.cumsum(window) - 1, count_all)
    listing = (
        jnp.zeros((count_all + 1,), jnp.int32)
        .at[places]
        .set(jnp.arange(count_all, dtype=jnp.int32))
    )
    return (listing[:count_all], jnp.sum(window))


def body(inverse, pattern, factor, diag_inverse):
    row_count = lax.axis_size(ROW)
    col_count = lax.axis_size("col")
    group_ratio = row_count // col_count
    my_column = lax.axis_index("col")
    tile_rows = inverse.shape[0] // B
    tile_cols = inverse.shape[1] // B
    first_row = lax.axis_index(ROW) * tile_rows
    gathered = gather_axes(factor, ROW, 0)
    arrived = lax.all_to_all(gathered, "col", split_axis=0, concat_axis=0, tiled=True)
    column_block = (
        arrived.reshape(col_count, group_ratio, factor.shape[0], W)
        .transpose(1, 0, 2, 3)
        .reshape(-1, W)
    )
    listing, mine_count = stored_list(
        pattern, first_row, my_column * tile_cols, tile_rows, tile_cols
    )

    def local_step(position, running):
        chosen = listing[position]
        tile_row = chosen // tile_cols
        tile_col = chosen % tile_cols
        inv_block = lax.dynamic_slice(inverse, (tile_row * B, tile_col * B), (B, B))
        rows_part = lax.dynamic_slice_in_dim(column_block, tile_col * B, B, 0)
        return add_product(running, tile_row, inv_block, rows_part)

    partial_sum = jnp.zeros((inverse.shape[0], W), jnp.float32)
    partial_sum = lax.fori_loop(0, mine_count, local_step, partial_sum)
    outer_local = None
    panel_sum = lax.psum_scatter(partial_sum, "col", scatter_dimension=0, tiled=True)
    outer_local = jnp.dot(factor.T, panel_sum, precision=HIGHEST)
    diag_block = diag_inverse + lax.psum(outer_local, ROW_COL)
    return (-panel_sum, diag_block)


def solution(mesh):
    finer = Mesh(mesh.devices.reshape(8, 2, mesh.shape["col"]), ("row_0", "row_1", "col"))
    return jax.shard_map(
        body,
        mesh=finer,
        in_specs=(P(ROW, "col"), P(), P(ROW_COL, None), P()),
        out_specs=(P(ROW_COL, None), P()),
        check_vma=False,
    )
```

profile of v0, /device:TPU:1, one launch (start us, length us, event | category | flops | bytes accessed | tf_op | source)
XLA Modules:
  0.0 661.3 jit_solution(15600625115745835680)
XLA Ops:
  7.2 0.0 all-gather.2.cloned.1.call-start
  7.2 14.5 %all_gather.6 = f32[192,1024]{1,0:T(8,128)} all-gather(f32[96,1024]{1,0:T(8,128)} %param.8), channel_id=1, replica_groups=mesh['row_0'=8,'row_1'=2,'col'=16] {'row_1'}, dimensions={0}, use_global_device_ids=true | all-gather | bytes 1179648 | tf_op jit(solution)/shard_map/all_gather | solution.py:19
  21.7 0.0 all-gather.2.cloned.1.call-update
  21.8 77.3 %all-gather.2.cloned.1.call-done = f32[1536,1024]{1,0:T(8,128)} async-done(((f32[192,1024]{1,0:T(8,128)}), f32[1536,1024]{1,0:T(8,128)}) %all-gather.2.cloned.1.call-update) | async-done | bytes 6291472 | tf_op jit(solution)/shard_map/all_gather | solution.py:19
  99.0 5.9 all-to-all-start
  104.9 0.0 reduce-scatter.2.cloned.1.call-start
  105.0 1.4 fusion.9
  106.4 0.1 reshape.47
  106.5 0.2 reduce-window.4
  106.6 0.6 scatter_custom_fusion
  107.3 86.2 %all-to-all-done = f32[16,96,1024]{2,1,0:T(8,128)} async-done(((f32[16,96,1024]{2,1,0:T(8,128)}), f32[16,96,1024]{2,1,0:T(8,128)}, u32[]{:S(2)}, u32[]{:S(2)}) %all-to-all-start) | async-done | bytes 6291488 | tf_op jit(solution)/shard_map/all_to_all | solution.py:51
  193.4 3.4 broadcast_in_dim.8
  196.9 32.6 %while.12 = (s32[]{:T(128)}, f32[1536,1024]{1,0:T(8,128)}, s32[]{:T(128)}, s32[9]{0:T(128)S(1)}, f32[1536,1536]{1,0:T(8,128)}, /*index=5*/f32[1536,1024]{1,0:T(8...) while((s32[]{:T(128)}, f32[1536,1024]{1,0:T(8,128)}, ...), condition=%wide.region_4.5_spmd, body=%wide.region_3.4_spmd.sunk | while | flops 3221749760 | bytes 7342474 | solution.py:70
  197.6 0.7 dynamic_slice.43
  200.1 7.4 %add_dynamic-update-slice_fusion.2 = f32[1536,1024]{1,0:T(8,128)} fusion(f32[1536,1024]{1,0:T(8,128)} %get-tuple-element.156, s32[]{:T(128)S(6)} %select_n.86, f32[1536,1024]{1,0:T(8,128)} %get-tuple-element.175, s32[]{:T(128)S(6)} %select_n.88, f32[1536,1536]{1,0:T(8,128)} %get-tuple-element.174), kind=kOutput, calls=%fused_computation.1.clone.1 | convolution fusion | flops 3221749760 | bytes 7342080 | tf_op jit(solution)/shard_map/while/body/dot_general | solution.py:26
  208.2 0.7 dynamic_slice.43
  210.8 7.4 %add_dynamic-update-slice_fusion.2 = f32[1536,1024]{1,0:T(8,128)} fusion(f32[1536,1024]{1,0:T(8,128)} %get-tuple-element.156, s32[]{:T(128)S(6)} %select_n.86, f32[1536,1024]{1,0:T(8,128)} %get-tuple-element.175, s32[]{:T(128)S(6)} %select_n.88, f32[1536,1536]{1,0:T(8,128)} %get-tuple-element.174), kind=kOutput, calls=%fused_computation.1.clone.1 | convolution fusion | flops 3221749760 | bytes 7342080 | tf_op jit(solution)/shard_map/while/body/dot_general | solution.py:26
  218.8 0.7 dynamic_slice.43
  221.4 7.4 %add_dynamic-update-slice_fusion.2 = f32[1536,1024]{1,0:T(8,128)} fusion(f32[1536,1024]{1,0:T(8,128)} %get-tuple-element.156, s32[]{:T(128)S(6)} %select_n.86, f32[1536,1024]{1,0:T(8,128)} %get-tuple-element.175, s32[]{:T(128)S(6)} %select_n.88, f32[1536,1536]{1,0:T(8,128)} %get-tuple-element.174), kind=kOutput, calls=%fused_computation.1.clone.1 | convolution fusion | flops 3221749760 | bytes 7342080 | tf_op jit(solution)/shard_map/while/body/dot_general | solution.py:26
  229.5 0.0 copy-start
  229.5 0.0 reduce-scatter.2.cloned.1.call-update
  229.5 0.0 all-reduce.2.cloned.1.call-start
  229.6 137.6 %reduce-scatter.2.cloned.1.call-done = f32[96,1024]{1,0:T(8,128)} async-done(((f32[1536,1024]{1,0:T(8,128)}), f32[96,1024]{1,0:T(8,128)}) %reduce-scatter.2.cloned.1.call-update) | async-done | bytes 393232 | tf_op jit(solution)/shard_map/reduce_scatter | solution.py:72
  367.2 0.0 copy-done
  367.2 6.1 convolution_bitcast_fusion
  373.4 0.0 copy-start.1
  373.4 0.0 all-reduce.2.cloned.1.call-update
  373.4 5.4 copy.6
  378.8 0.0 copy-done.1
  378.8 0.8 neg.3
  379.6 263.1 %all-reduce.2.cloned.1.call-done = f32[1024,1024]{0,1:T(8,128)} async-done(((f32[1024,1024]{0,1:T(8,128)}), f32[1024,1024]{0,1:T(8,128)}) %all-reduce.2.cloned.1.call-update) | async-done | bytes 4194320 | tf_op jit(solution)/shard_map/psum | solution.py:74
  642.7 6.8 %add.82 = f32[1024,1024]{0,1:T(8,128)} add(f32[1024,1024]{0,1:T(8,128)} %copy.6, f32[1024,1024]{0,1:T(8,128)} %all-reduce.2.cloned.1.call-done) | non-fusion elementwise | flops 1048576 | bytes 12582912 | tf_op jit(solution)/shard_map/add | solution.py:74
  649.5 5.3 copy.7
  (2 shorter events, 0.0 us)
Async XLA Ops:
  7.2 91.9 %all-gather.2.cloned.1.call-start = ((), (), s32[]{:S(2)}) async-start(), calls=%async_computation.2 | async-start | bytes 7077888 | tf_op jit(solution)/shard_map/all_gather | solution.py:19
  99.0 94.4 %all-to-all-start = ((f32[16,96,1024]{2,1,0:T(8,128)}), f32[16,96,1024]{2,1,0:T(8,128)}, u32[]{:S(2)}, u32[]{:S(2)}) async-start(f32[16,96,1024]{2,1,0:T(8,128)} %bitcast.18), calls=%async_computation | async-start | bytes 12582912 | tf_op jit(solution)/shard_map/all_to_all | solution.py:51
  104.9 262.3 %reduce-scatter.2.cloned.1.call-start = ((), (), s32[]{:S(2)}) async-start(), calls=%async_computation.3 | async-start | bytes 6684672 | tf_op jit(solution)/shard_map/reduce_scatter | solution.py:72
  229.5 137.7 %copy-start = (f32[96,1024]{1,0:T(8,128)S(1)}, f32[96,1024]{1,0:T(8,128)}, u32[]{:S(2)}) copy-start(f32[96,1024]{1,0:T(8,128)} %param.8) | copy-start | bytes 1179652
  229.5 413.1 %all-reduce.2.cloned.1.call-start = ((), (), s32[]{:S(2)}) async-start(), calls=%async_computation.4 | async-start | bytes 8388608 | tf_op jit(solution)/shard_map/psum | solution.py:74
  373.4 5.4 copy-start.1
Sparse Core Ops, SparseCore 0:
  21.9 77.0 all-gather.1
  229.6 137.5 reduce-scatter.1
  373.5 269.1 all-reduce.1
where the time goes:
time: 663 us; the launch traced here: 661 us
  waiting for transfers between devices  564 us (85%)
  matrix products  28.4 us (4%)
  local copies, waits for them, and re-layouts  16.8 us (3%)
  blocking collectives  14.5 us (2%)
  between operations  13.8 us (2%)
  other arithmetic  9.18 us (1%)
  loops' own time  8.36 us (1%)
    psum x1, waiting for transfers between devices, body(): diag_block = diag_inverse + lax.psum(outer_local, ROW_COL)  263 us
    reduce_scatter x1, waiting for transfers between devices, body(): lax.psum_scatter(partial_sum, 'col', scatter_dimension=0, tiled=True)  138 us
    all_to_all x1, waiting for transfers between devices, body(): lax.all_to_all(gathered, 'col', split_axis=0, concat_axis=0, tiled=True)  86.2 us
    all_gather x1, waiting for transfers between devices, gather_axes(): nearer = lax.all_gather(value, axes[-1], axis=dim, tiled=True)  77.3 us
    dot_general x3, matrix products, add_product(): update = current + jnp.dot(inv_block, rows_part, precision=HIGHEST)  22.3 us
    all_gather x1, blocking collectives, gather_axes(): nearer = lax.all_gather(value, axes[-1], axis=dim, tiled=True)  14.5 us
  transfers between devices with their start and end apart: 4, of which 4 were waited for; matrix products, arithmetic and copies ran while one was open for 1% of the time, Pallas kernels for 0%

commit v1 on v0

v1 whole, which is shorter than its diff:
```python
import functools

import jax
import jax.numpy as jnp
from jax import lax
from jax.experimental import pallas as pl
from jax.experimental.pallas import tpu as pltpu
from jax.sharding import PartitionSpec as P

MESH = pl.DeviceIdType.MESH
F32 = jnp.float32
BF16 = jnp.bfloat16

FULL = {"NZ": 8, "XH": 2, "XL": 2, "NY": 4, "W": 1024, "CH": 256, "RB": 96, "B": 512}
STAGES = {"rx": 8, "ry": 11, "dot": 13, "dy": 15, "dx": 17, "dz": 19, "az": 22, "ax": 24, "ay": 26, "ac": 27, "out": 28}


def split(value):
    high = value.astype(BF16)
    return high, (value - high.astype(F32)).astype(BF16)


def kernel(
    g, inv_hbm, pat_ref, fac_ref, dinv_hbm, panel_ref, diag_hbm,
    stage, ih, il, gath, fh, fl, part, rc, rx, ry, fth, ftl, dpart, dc, dy, dx, dz, full, dinv,
    load_sem, got, src_sem, fwd_sem, rc_s, rc_r, rx_s, rx_r, ry_s, ry_r, dc_s, dc_r, dy_s, dy_r, dx_s, dx_r,
    dz_s, dz_r, az_s, az_r, ax_s, ax_r, ay_s, ay_r, ac_s, ac_r, out_sem,
):
    nz, xhn, xln, ny, w, ch, rb = (g[k] for k in ("NZ", "XH", "XL", "NY", "W", "CH", "RB"))
    nx, chunks, ncol = xhn * xln, w // ch, xln * ny * 2
    half = rb // 2
    row, col = lax.axis_index("row"), lax.axis_index("col")
    z, xh = row // xhn, row % xhn
    core, y, xl = col % 2, (col // 2) % ny, col // (2 * ny)
    x = xh * xln + xl

    def at(z_, x_, y_, core_):
        return (z_ * xhn + x_ // xln, (x_ % xln) * (2 * ny) + y_ * 2 + core_)

    def z_peer(j):
        return at(lax.rem(z + j, nz), x, y, core)

    def x_peer(j):
        return at(z, lax.rem(x + j, nx), y, core)

    def y_peer(j):
        return at(z, x, lax.rem(y + j, ny), core)

    sibling = at(z, x, y, 1 - core)
    x_next = at(z, xh * xln + (xln - 1 - xl), y, core)
    z_root = col // 2
    up = lax.rem(z - z_root + nz, nz)
    down = lax.rem(nz - up, nz)
    is_root = up == 0
    on_diag = row == col

    def remote(src, dst, send, recv, dev):
        return pltpu.make_async_remote_copy(
            src_ref=src, dst_ref=dst, send_sem=send, recv_sem=recv, device_id=dev, device_id_type=MESH
        )

    def landed(ref, recv):
        remote(ref, ref, recv, recv, sibling).wait_recv()

    def sent(ref, send):
        remote(ref, ref, send, send, sibling).wait_send()

    load = pltpu.make_async_copy(inv_hbm, stage, load_sem.at[0])
    load.start()
    d_half, d_y, d_x = w // 2, w // 2 // ny, w // 2 // ny // nx
    lanes = ch // 128
    d_z = d_x * lanes // nz
    y_base = core * d_half + y * d_y
    x_base = y_base + x * d_x

    def z_place(z_):
        first = pl.multiple_of(x_base + (z_ // lanes) * d_z, d_z)
        return pl.ds(first, d_z), pl.ds(pl.multiple_of((z_ % lanes) * 128, 128), 128)

    def rows_of(first, size):
        return pl.ds(pl.multiple_of(first, size), size)

    z_rows, z_lanes = z_place(z)

    def dinv_copy(k):
        first = pl.multiple_of(k * ch + (z % lanes) * 128, 128)
        return pltpu.make_async_copy(dinv_hbm.at[z_rows, pl.ds(first, 128)], dinv.at[k], load_sem.at[1 + k])

    for k in range(chunks):
        dinv_copy(k).start()

    barrier = pltpu.get_barrier_semaphore()

    def greet(dev):
        pl.semaphore_signal(barrier, inc=1, device_id=dev, device_id_type=MESH)

    greet(sibling)
    for j in range(1, nz):
        greet(z_peer(j))
    for j in range(1, nx):
        greet(x_peer(j))
    for j in range(1, ny):
        greet(y_peer(j))
    others = 1 + (nz - 1) + (nx - 1) + (ny - 1)
    for a in range(xhn):
        pl.when(jnp.logical_not(jnp.logical_and(on_diag, xh == a)))(lambda a=a: greet((z * xhn + a, row)))

    @pl.when(is_root)
    def _():
        @pl.loop(0, ncol)
        def _(j):
            pl.when(jnp.logical_not(jnp.logical_and(on_diag, j == col)))(lambda: greet((z * xhn + core, j)))

    mine = jnp.where(on_diag, 1, 0)
    pl.semaphore_wait(barrier, others + xhn - mine + jnp.where(is_root, ncol - mine, 0))

    def send_source(k):
        for a in range(xhn):
            here = jnp.logical_and(on_diag, xh == a)
            for way in range(2):
                src = fac_ref.at[pl.ds(way * half, half), pl.ds(pl.multiple_of(k * ch, ch), ch)]
                dst = gath.at[way, k, col]

                @pl.when(jnp.logical_not(here))
                def _(src=src, dst=dst, way=way, a=a):
                    remote(src, dst, src_sem, got.at[way, k, col], (z * xhn + a, row)).start()

                @pl.when(here)
                def _(src=src, dst=dst, way=way):
                    pltpu.make_async_copy(src, dst, got.at[way, k, col]).start()

    for k in range(min(2, chunks)):
        send_source(k)
    turned = fac_ref[...].T
    fth[...], ftl[...] = split(turned)
    load.wait()

    def mask_rows(i):
        block, part_of = i // (rb // 32), i % (rb // 32)
        dest = rows_of(((block % 2) * (ncol // 2) + block // 2) * rb + part_of * 32, 32)
        tiles = (rb * ncol) // g["B"]
        tile_row = (i * 32) // g["B"]
        for j in range(tiles):
            keep = pat_ref[row * tiles + tile_row, col * tiles + j].astype(F32)
            cols = pl.ds(j * g["B"], g["B"])
            ih[dest, cols], il[dest, cols] = split(stage[rows_of(i * 32, 32), cols] * keep)

    per = ncol // 4

    def gather_step(k, h):
        @pl.loop(0, per)
        def _(n):
            i = h * per + n
            for way, far, step in ((0, up, 1), (1, down, nz - 1)):
                piece = gath.at[way, k, i]
                landed(piece, got.at[way, k, i])
                pl.when(far < nz - 1)(
                    lambda piece=piece, way=way, step=step: remote(
                        piece, piece, fwd_sem.at[way], got.at[way, k, i], z_peer(step)
                    ).start()
                )
                rows = rows_of(i * rb + way * half, half)
                fh[k, rows, :], fl[k, rows, :] = split(gath[way, k, i])

    m = rb * ncol // 4
    mine_rows = rb * ncol // 2

    def product(k, h):
        rows = rows_of(h * m, m)
        left_h, left_l = ih[rows, :], il[rows, :]
        right_h, right_l = fh[k], fl[k]
        total = jnp.dot(left_h, right_h, preferred_element_type=F32)
        total += jnp.dot(left_h, right_l, preferred_element_type=F32)
        total += jnp.dot(left_l, right_h, preferred_element_type=F32)
        part[k, rows, :] = total

    def rc_send(k):
        remote(part.at[k, rows_of((1 - core) * mine_rows, mine_rows)], rc.at[k], rc_s, rc_r.at[k], sibling).start()

    core_base = core * mine_rows
    x_rows = mine_rows // xln

    def rx_stage(k):
        landed(rc.at[k], rc_r.at[k])
        own = rows_of(core_base, mine_rows)
        part[k, own, :] += rc[k]
        if xln > 1:
            remote(part.at[k, rows_of(core_base + (1 - xl) * x_rows, x_rows)], rx.at[k], rx_s, rx_r.at[k], x_next).start()

    def ry_stage(k):
        base = core_base + xl * x_rows
        if xln > 1:
            landed(rx.at[k], rx_r.at[k])
            own = rows_of(base, x_rows)
            part[k, own, :] += rx[k]
        for j in range(1, ny):
            rows = rows_of(base + lax.rem(y + j, ny) * rb, rb)
            remote(part.at[k, rows], ry.at[k, j - 1], ry_s, ry_r.at[k], y_peer(j)).start()

    def dot_stage(k):
        landed(ry.at[k], ry_r.at[k])
        total = part[k, rows_of(core_base + xl * x_rows + y * rb, rb), :]
        for j in range(ny - 1):
            total += ry[k, j]
        panel_ref[k] = -total
        right_h, right_l = split(total)
        update = jnp.dot(fth[...], right_h, preferred_element_type=F32)
        update += jnp.dot(fth[...], right_l, preferred_element_type=F32)
        update += jnp.dot(ftl[...], right_h, preferred_element_type=F32)
        dpart[k] = update
        remote(dpart.at[k, rows_of((1 - core) * d_half, d_half)], dc.at[k], dc_s, dc_r.at[k], sibling).start()

    def dy_stage(k):
        landed(dc.at[k], dc_r.at[k])
        dpart[k, rows_of(core * d_half, d_half), :] += dc[k]
        for j in range(1, ny):
            rows = rows_of(core * d_half + lax.rem(y + j, ny) * d_y, d_y)
            remote(dpart.at[k, rows], dy.at[k, j - 1], dy_s, dy_r.at[k], y_peer(j)).start()

    def dx_stage(k):
        landed(dy.at[k], dy_r.at[k])
        own = rows_of(y_base, d_y)
        dpart[k, own, :] += functools.reduce(lambda a, b: a + b, [dy[k, j] for j in range(ny - 1)])
        for j in range(1, nx):
            rows = rows_of(y_base + lax.rem(x + j, nx) * d_x, d_x)
            remote(dpart.at[k, rows], dx.at[k, j - 1], dx_s, dx_r.at[k], x_peer(j)).start()

    def dz_stage(k):
        landed(dx.at[k], dx_r.at[k])
        own = rows_of(x_base, d_x)
        dpart[k, own, :] += functools.reduce(lambda a, b: a + b, [dx[k, j] for j in range(nx - 1)])
        for j in range(1, nz):
            rows, cols = z_place(lax.rem(z + j, nz))
            remote(dpart.at[k, rows, cols], dz.at[k, j - 1], dz_s, dz_r.at[k], z_peer(j)).start()

    def az_stage(k):
        landed(dz.at[k], dz_r.at[k])
        total = dpart[k, z_rows, z_lanes] + dinv[k]
        for j in range(nz - 1):
            total += dz[k, j]
        full[k, z_rows, z_lanes] = total
        place = full.at[k, z_rows, z_lanes]
        for j in range(1, nz):
            remote(place, place, az_s, az_r.at[k], z_peer(j)).start()

    def ax_stage(k):
        landed(dz.at[k], az_r.at[k])
        place = full.at[k, rows_of(x_base, d_x)]
        for j in range(1, nx):
            remote(place, place, ax_s, ax_r.at[k], x_peer(j)).start()

    def ay_stage(k):
        landed(dx.at[k], ax_r.at[k])
        place = full.at[k, rows_of(y_base, d_y)]
        for j in range(1, ny):
            remote(place, place, ay_s, ay_r.at[k], y_peer(j)).start()

    def ac_stage(k):
        landed(dy.at[k], ay_r.at[k])
        place = full.at[k, rows_of(core * d_half, d_half)]
        remote(place, place, ac_s, ac_r.at[k], sibling).start()

    def out_copy(k):
        cols = pl.ds(pl.multiple_of(k * ch, ch), ch)
        return pltpu.make_async_copy(full.at[k], diag_hbm.at[:, cols], out_sem.at[k])

    def out_stage(k):
        landed(dc.at[k], ac_r.at[k])
        out_copy(k).start()

    for k in range(chunks):
        dinv_copy(k).wait()

    stages = {
        "rx": rx_stage, "ry": ry_stage, "dot": dot_stage, "dy": dy_stage, "dx": dx_stage, "dz": dz_stage,
        "az": az_stage, "ax": ax_stage, "ay": ay_stage, "ac": ac_stage, "out": out_stage,
    }
    masks = rb * ncol // 32 // 4

    @pl.loop(0, 4 * (chunks - 1) + STAGES["out"] + 1)
    def _(u):
        k, h = u // 4, u % 4

        @pl.when(u < 4 * chunks)
        def _():
            pl.when(jnp.logical_and(h == 0, k + 2 < chunks))(lambda: send_source(k + 2))
            gather_step(k, h)

        @pl.when(u < 4)
        def _():
            @pl.loop(0, masks)
            def _(n):
                mask_rows(u * masks + n)

        @pl.when(jnp.logical_and(u >= 4, u < 4 * chunks + 4))
        def _():
            product(k - 1, h)
            pl.when(h == 3)(lambda: rc_send(k - 1))

        for name, after in sorted(STAGES.items(), key=lambda item: -item[1]):
            since = u - after
            runs = jnp.logical_and(h == after % 4, jnp.logical_and(since >= 0, since < 4 * chunks))
            pl.when(runs)(lambda name=name, since=since: stages[name](since // 4))

    for k in range(chunks):
        out_copy(k).wait()
    sent(fac_ref, src_sem)
    pl.when(jnp.logical_not(on_diag))(lambda: sent(fac_ref, src_sem))
    pl.when(up < nz - 1)(lambda: sent(gath.at[0], fwd_sem.at[0]))
    pl.when(down < nz - 1)(lambda: sent(gath.at[1], fwd_sem.at[1]))
    sent(rc, rc_s)
    if xln > 1:
        sent(rx, rx_s)
    for ref, sem in ((ry, ry_s), (dc, dc_s), (dy, dy_s), (dx, dx_s), (dz, dz_s), (dz, az_s), (dx, ax_s), (dy, ay_s), (dc, ac_s)):
        sent(ref, sem)


def make(g):
    nz, xhn, xln, ny, w, ch, rb = (g[k] for k in ("NZ", "XH", "XL", "NY", "W", "CH", "RB"))
    nx, chunks, ncol = xhn * xln, w // ch, xln * ny * 2
    n = rb * ncol
    dma = pltpu.SemaphoreType.DMA
    d_half, d_y, d_x = w // 2, w // 2 // ny, w // 2 // ny // nx
    d_z = d_x * (ch // 128) // nz

    def body(inverse, pattern, factor, diag_inverse):
        panel, diag = pl.pallas_call(
            functools.partial(kernel, g),
            out_shape=(jax.ShapeDtypeStruct((chunks, rb, ch), F32), jax.ShapeDtypeStruct((w, w), F32)),
            in_specs=[
                pl.BlockSpec(memory_space=pl.ANY),
                pl.BlockSpec(memory_space=pltpu.SMEM),
                pl.BlockSpec(memory_space=pltpu.VMEM),
                pl.BlockSpec(memory_space=pl.ANY),
            ],
            out_specs=(pl.BlockSpec(memory_space=pltpu.VMEM), pl.BlockSpec(memory_space=pl.ANY)),
            scratch_shapes=[
                pltpu.VMEM((n, n), F32),
                pltpu.VMEM((n, n), BF16),
                pltpu.VMEM((n, n), BF16),
                pltpu.VMEM((2, chunks, ncol, rb // 2, ch), F32),
                pltpu.VMEM((chunks, n, ch), BF16),
                pltpu.VMEM((chunks, n, ch), BF16),
                pltpu.VMEM((chunks, n, ch), F32),
                pltpu.VMEM((chunks, n // 2, ch), F32),
                pltpu.VMEM((chunks, n // 2 // xln, ch), F32),
                pltpu.VMEM((chunks, ny - 1, rb, ch), F32),
                pltpu.VMEM((w, rb), BF16),
                pltpu.VMEM((w, rb), BF16),
                pltpu.VMEM((chunks, w, ch), F32),
                pltpu.VMEM((chunks, d_half, ch), F32),
                pltpu.VMEM((chunks, ny - 1, d_y, ch), F32),
                pltpu.VMEM((chunks, nx - 1, d_x, ch), F32),
                pltpu.VMEM((chunks, nz - 1, d_z, 128), F32),
                pltpu.VMEM((chunks, w, ch), F32),
                pltpu.VMEM((chunks, d_z, 128), F32),
                dma((1 + chunks,)),
                dma((2, chunks, ncol)),
                dma,
                dma((2,)),
            ]
            + [dma, dma((chunks,))] * 11
            + [dma((chunks,))],
            compiler_params=pltpu.CompilerParams(
                collective_id=0, has_side_effects=True, vmem_limit_bytes=63 * 2**20
            ),
        )(inverse, pattern, factor, diag_inverse)
        return panel.transpose(1, 0, 2).reshape(rb, w), diag

    return body


def solution(mesh):
    return jax.shard_map(
        make(FULL),
        mesh=mesh,
        in_specs=(P("row", "col"), P(), P(("row", "col"), None), P()),
        out_specs=(P(("row", "col"), None), P()),
        check_vma=False,
    )
```

time: 663 us -> 2700 us (4.07)
  Pallas kernels: 0 us -> 2690 us
  waiting for transfers between devices: 564 us -> 0 us
  matrix products: 28.4 us -> 0 us
    pallas_call x0 -> x1, Pallas kernels: none -> 2690 us  [body(): pl.pallas_call(functools.partial(kernel, g), out_shape=(jax.ShapeDtypeStr...]
    psum x1 -> x0, waiting for transfers between devices: 263 us -> none  [body(): diag_block = diag_inverse + lax.psum(outer_local, ROW_COL)]
    reduce_scatter x1 -> x0, waiting for transfers between devices: 138 us -> none  [body(): lax.psum_scatter(partial_sum, 'col', scatter_dimension=0, tiled=True)]
    all_to_all x1 -> x0, waiting for transfers between devices: 86.2 us -> none  [body(): lax.all_to_all(gathered, 'col', split_axis=0, concat_axis=0, tiled=True)]
    all_gather x1 -> x0, waiting for transfers between devices: 77.3 us -> none  [gather_axes(): nearer = lax.all_gather(value, axes[-1], axis=dim, tiled=True)]
    dot_general x4 -> x0, matrix products: 28.4 us -> none  [the longest x3 22.3 us: add_product(): update = current + jnp.dot(inv_block, rows_part, precision=HIGHEST)]
  transfers between devices with their start and end apart: 4 -> 0, of which waited for: 4 -> 0; matrix products, arithmetic and copies ran while one was open for 1% -> 0% of each run, Pallas kernels for 0% -> 0%
where the time goes in v1:
time: 2700 us
  Pallas kernels  2690 us (100%)
    pallas_call x1, Pallas kernels, body(): pl.pallas_call(functools.partial(kernel, g), out_shape=(jax.ShapeDtypeStr...  2690 us

profile of v1, /device:TPU:1, one launch (start us, length us, event | category | flops | bytes accessed | tf_op | source)
XLA Modules:
  0.0 2698.7 jit_solution(4088442463198125939)
XLA Ops:
  0.6 2691.5 %shard_map.59 = (f32[4,96,256]{2,1,0:T(8,128)}, f32[1024,1024]{1,0:T(8,128)}) custom-call(f32[1536,1536]{1,0:T(8,128)} %inv_hbm.1, s32[48,48]{1,0:T(8,128)} %pat_ref.1, f32[96,1024]{1,0:T(8,128)} %fac_ref.1, f32[1024,1024]{1,0:T(8,128)} %dinv_hbm.1), custom_call_target="tpu_custom_call" | custom-call | tf_op jit(solution)/shard_map/pallas_call | solution.py:327
  2692.1 1.8 copy.7
  2693.9 4.8 copy.9

commit v2 on v1

--- a/solution.py
+++ b/solution.py
@@ -12,7 +12,8 @@
 BF16 = jnp.bfloat16
 
 FULL = {"NZ": 8, "XH": 2, "XL": 2, "NY": 4, "W": 1024, "CH": 256, "RB": 96, "B": 512}
-STAGES = {"rx": 8, "ry": 11, "dot": 13, "dy": 15, "dx": 17, "dz": 19, "az": 22, "ax": 24, "ay": 26, "ac": 27, "out": 28}
+STAGES = {'rx': 1, 'ry': 4, 'dot': 7, 'dy': 8, 'dx': 11, 'dz': 13, 'az': 15, 'ax': 17, 'ay': 19, 'ac': 22, 'out': 23}
+HOP = 5
 
 
 def split(value):
@@ -147,18 +148,22 @@
 
     per = ncol // 4
 
-    def gather_step(k, h):
-        @pl.loop(0, per)
-        def _(n):
-            i = h * per + n
-            for way, far, step in ((0, up, 1), (1, down, nz - 1)):
+    pieces = chunks * ncol
+
+    def gather_step(t):
+        for way, far, step in ((0, up, 1), (1, down, nz - 1)):
+            p = t - HOP * far
+
+            @pl.when(jnp.logical_and(p >= 0, p < pieces))
+            def _(way=way, far=far, step=step, p=p):
+                k, i = p // ncol, p % ncol
                 piece = gath.at[way, k, i]
                 landed(piece, got.at[way, k, i])
-                pl.when(far < nz - 1)(
-                    lambda piece=piece, way=way, step=step: remote(
-                        piece, piece, fwd_sem.at[way], got.at[way, k, i], z_peer(step)
-                    ).start()
-                )
+
+                @pl.when(far < nz - 1)
+                def _():
+                    remote(piece, piece, fwd_sem.at[way], got.at[way, k, i], z_peer(step)).start()
+
                 rows = rows_of(i * rb + way * half, half)
                 fh[k, rows, :], fl[k, rows, :] = split(gath[way, k, i])
 
@@ -277,14 +282,17 @@
     }
     masks = rb * ncol // 32 // 4
 
-    @pl.loop(0, 4 * (chunks - 1) + STAGES["out"] + 1)
+    ready = (ncol - 1 + HOP * (nz - 1)) // per + 1
+
+    @pl.loop(0, 4 * chunks + ready + 3 + STAGES["out"])
     def _(u):
-        k, h = u // 4, u % 4
-
-        @pl.when(u < 4 * chunks)
+        @pl.when(u < 4 * (chunks - 1) + ready)
         def _():
-            pl.when(jnp.logical_and(h == 0, k + 2 < chunks))(lambda: send_source(k + 2))
-            gather_step(k, h)
+            pl.when(jnp.logical_and(u % 4 == 0, u // 4 + 2 < chunks))(lambda: send_source(u // 4 + 2))
+
+            @pl.loop(0, per)
+            def _(n):
+                gather_step(u * per + n)
 
         @pl.when(u < 4)
         def _():
@@ -292,14 +300,16 @@
             def _(n):
                 mask_rows(u * masks + n)
 
-        @pl.when(jnp.logical_and(u >= 4, u < 4 * chunks + 4))
+        since = u - ready
+
+        @pl.when(jnp.logical_and(since >= 0, since < 4 * chunks))
         def _():
-            product(k - 1, h)
-            pl.when(h == 3)(lambda: rc_send(k - 1))
+            product(since // 4, since % 4)
+            pl.when(since % 4 == 3)(lambda: rc_send(since // 4))
 
         for name, after in sorted(STAGES.items(), key=lambda item: -item[1]):
-            since = u - after
-            runs = jnp.logical_and(h == after % 4, jnp.logical_and(since >= 0, since < 4 * chunks))
+            since = u - ready - 3 - after
+            runs = jnp.logical_and(since % 4 == 0, jnp.logical_and(since >= 0, since < 4 * chunks))
             pl.when(runs)(lambda name=name, since=since: stages[name](since // 4))
 
     for k in range(chunks):

time: 2700 us -> 241 us (0.09)
  Pallas kernels: 2690 us -> 234 us
    pallas_call x1, Pallas kernels: 2690 us -> 234 us  [body(): pl.pallas_call(functools.partial(kernel, g), out_shape=(jax.ShapeDtypeStr...]
where the time goes in v2:
time: 241 us
  Pallas kernels  234 us (97%)
  local copies, waits for them, and re-layouts  6.57 us (3%)
    pallas_call x1, Pallas kernels, body(): pl.pallas_call(functools.partial(kernel, g), out_shape=(jax.ShapeDtypeStr...  234 us

profile of v2, /device:TPU:1, one launch (start us, length us, event | category | flops | bytes accessed | tf_op | source)
XLA Modules:
  0.0 241.2 jit_solution(2402273484623224885)
XLA Ops:
  0.6 234.0 %shard_map.59 = (f32[4,96,256]{2,1,0:T(8,128)}, f32[1024,1024]{1,0:T(8,128)}) custom-call(f32[1536,1536]{1,0:T(8,128)} %inv_hbm.1, s32[48,48]{1,0:T(8,128)} %pat_ref.1, f32[96,1024]{1,0:T(8,128)} %fac_ref.1, f32[1024,1024]{1,0:T(8,128)} %dinv_hbm.1), custom_call_target="tpu_custom_call" | custom-call | tf_op jit(solution)/shard_map/pallas_call | solution.py:337
  234.6 1.8 copy.7
  236.4 4.8 %copy.9 = f32[1024,1024]{1,0:T(8,128)} copy(f32[1024,1024]{1,0:T(8,128)} %get-tuple-element.9) | data formatting | bytes 8388608

commit v3 on v2

v3 whole, which is shorter than its diff:
```python
import functools

import jax
import jax.numpy as jnp
from jax import lax
from jax.experimental import pallas as pl
from jax.experimental.pallas import tpu as pltpu
from jax.sharding import PartitionSpec as P

MESH = pl.DeviceIdType.MESH
F32 = jnp.float32
BF16 = jnp.bfloat16

FULL = {"NZ": 8, "XH": 2, "XL": 2, "NY": 4, "W": 1024, "CH": 128, "RB": 96, "B": 512}
STAGES = {"ry": 1, "dot": 5, "dp": 7, "dz": 10, "ap": 12, "ac": 15, "out": 16}
HOP = 4
AHEAD = 1


def split(value):
    high = value.astype(BF16)
    return high, (value - high.astype(F32)).astype(BF16)


def kernel(
    g, inv_hbm, pat_ref, fac_ref, dinv_hbm, panel_ref, diag_hbm,
    stage, ih, il, gath, fh, fl, part, rc, ry, fth, ftl, dpart, dc, dp, dz, full, dinv,
    load_sem, got, src_sem, fwd_sem, rc_s, rc_r, ry_s, ry_r, dc_s, dc_r, dp_s, dp_r,
    dz_s, dz_r, ap_s, ap_r, ac_s, ac_r, out_sem,
):
    nz, xhn, xln, ny, w, ch, rb = (g[k] for k in ("NZ", "XH", "XL", "NY", "W", "CH", "RB"))
    nx, chunks, ncol = xhn * xln, w // ch, xln * ny * 2
    per_way = ncol // 2
    row, col = lax.axis_index("row"), lax.axis_index("col")
    z, xh = row // xhn, row % xhn
    core, y, xl = col % 2, (col // 2) % ny, col // (2 * ny)
    x = xh * xln + xl

    def at(z_, x_, y_, core_):
        return (z_ * xhn + x_ // xln, (x_ % xln) * (2 * ny) + y_ * 2 + core_)

    def z_peer(j):
        return at(lax.rem(z + j, nz), x, y, core)

    def plane_peer(j):
        return at(z, lax.rem(x + j // ny, nx), lax.rem(y + j % ny, ny), core)

    def row_peer(j):
        return at(z, xh * xln + lax.rem(xl + j // ny, xln), lax.rem(y + j % ny, ny), core)

    sibling = at(z, x, y, 1 - core)
    z_root = col // 2
    up = lax.rem(z - z_root + nz, nz)
    down = lax.rem(nz - up, nz)
    is_root = up == 0
    on_diag = row == col

    def remote(src, dst, send, recv, dev):
        return pltpu.make_async_remote_copy(
            src_ref=src, dst_ref=dst, send_sem=send, recv_sem=recv, device_id=dev, device_id_type=MESH
        )

    def landed(ref, recv):
        remote(ref, ref, recv, recv, sibling).wait_recv()

    def sent(ref, send):
        remote(ref, ref, send, send, sibling).wait_send()

    load = pltpu.make_async_copy(inv_hbm, stage, load_sem.at[0])
    load.start()
    d_half, d_rows = w // 2, w // 2 // (nx * ny)

    def rows_of(first, size):
        return pl.ds(pl.multiple_of(first, size), size)

    mine_d = rows_of(core * d_half + (x * ny + y) * d_rows, d_rows)

    def dinv_copy(k):
        cols = pl.ds(pl.multiple_of(k * ch, ch), ch)
        return pltpu.make_async_copy(dinv_hbm.at[mine_d, cols], dinv.at[k], load_sem.at[1 + k])

    for k in range(chunks):
        dinv_copy(k).start()

    barrier = pltpu.get_barrier_semaphore()

    def greet(dev):
        pl.semaphore_signal(barrier, inc=1, device_id=dev, device_id_type=MESH)

    greet(sibling)
    for j in range(1, nz):
        greet(z_peer(j))
    for j in range(1, nx * ny):
        greet(plane_peer(j))
    others = 1 + (nz - 1) + (nx * ny - 1)
    for a in range(xhn):
        pl.when(jnp.logical_not(jnp.logical_and(on_diag, xh == a)))(lambda a=a: greet((z * xhn + a, row)))

    @pl.when(is_root)
    def _():
        @pl.loop(0, ncol)
        def _(j):
            pl.when(jnp.logical_not(jnp.logical_and(on_diag, j == col)))(lambda: greet((z * xhn + core, j)))

    mine = jnp.where(on_diag, 1, 0)
    pl.semaphore_wait(barrier, others + xhn - mine + jnp.where(is_root, ncol - mine, 0))

    def send_source(k):
        src = fac_ref.at[:, pl.ds(pl.multiple_of(k * ch, ch), ch)]
        dst = gath.at[k, col]
        for a in range(xhn):
            here = jnp.logical_and(on_diag, xh == a)
            pl.when(jnp.logical_not(here))(
                lambda a=a: remote(src, dst, src_sem, got.at[k, col], (z * xhn + a, row)).start()
            )
            pl.when(here)(lambda: pltpu.make_async_copy(src, dst, got.at[k, col]).start())

    for k in range(min(AHEAD, chunks)):
        send_source(k)
    turned = fac_ref[...].T
    fth[...], ftl[...] = split(turned)
    load.wait()

    def mask_rows(i):
        block, part_of = i // (rb // 32), i % (rb // 32)
        dest = rows_of(((block % 2) * (ncol // 2) + block // 2) * rb + part_of * 32, 32)
        tiles = (rb * ncol) // g["B"]
        tile_row = (i * 32) // g["B"]
        for j in range(tiles):
            keep = pat_ref[row * tiles + tile_row, col * tiles + j].astype(F32)
            cols = pl.ds(j * g["B"], g["B"])
            ih[dest, cols], il[dest, cols] = split(stage[rows_of(i * 32, 32), cols] * keep)


    pieces = chunks * per_way

    def gather_step(t):
        for way, far, step in ((0, up, 1), (1, down, nz - 1)):
            p = t - HOP * far

            @pl.when(jnp.logical_and(p >= 0, p < pieces))
            def _(way=way, far=far, step=step, p=p):
                k, i = p // per_way, way * per_way + p % per_way
                piece = gath.at[k, i]
                landed(piece, got.at[k, i])

                @pl.when(far < nz - 1)
                def _():
                    remote(piece, piece, fwd_sem.at[way], got.at[k, i], z_peer(step)).start()

                rows = rows_of(i * rb, rb)
                fh[k, rows, :], fl[k, rows, :] = split(gath[k, i])

    m = rb * ncol // 4
    mine_rows = rb * ncol // 2

    def product(k, h):
        rows = rows_of(h * m, m)
        left_h, left_l = ih[rows, :], il[rows, :]
        right_h, right_l = fh[k], fl[k]
        total = jnp.dot(left_h, right_h, preferred_element_type=F32)
        total += jnp.dot(left_h, right_l, preferred_element_type=F32)
        total += jnp.dot(left_l, right_h, preferred_element_type=F32)
        part[k, rows, :] = total

    def rc_send(k):
        remote(part.at[k, rows_of((1 - core) * mine_rows, mine_rows)], rc.at[k], rc_s, rc_r.at[k], sibling).start()

    core_base = core * mine_rows
    def ry_stage(k):
        landed(rc.at[k], rc_r.at[k])
        part[k, rows_of(core_base, mine_rows), :] += rc[k]
        for j in range(1, xln * ny):
            place = lax.rem(xl + j // ny, xln) * ny + lax.rem(y + j % ny, ny)
            rows = rows_of(core_base + place * rb, rb)
            remote(part.at[k, rows], ry.at[k, j - 1], ry_s, ry_r.at[k], row_peer(j)).start()

    def dot_stage(k):
        landed(ry.at[k], ry_r.at[k])
        total = part[k, rows_of(core_base + (xl * ny + y) * rb, rb), :]
        for j in range(xln * ny - 1):
            total += ry[k, j]
        panel_ref[k] = -total
        right_h, right_l = split(total)
        update = jnp.dot(fth[...], right_h, preferred_element_type=F32)
        update += jnp.dot(fth[...], right_l, preferred_element_type=F32)
        update += jnp.dot(ftl[...], right_h, preferred_element_type=F32)
        dpart[k] = update
        remote(dpart.at[k, rows_of((1 - core) * d_half, d_half)], dc.at[k], dc_s, dc_r.at[k], sibling).start()

    def dp_stage(k):
        landed(dc.at[k], dc_r.at[k])
        dpart[k, rows_of(core * d_half, d_half), :] += dc[k]
        for j in range(1, nx * ny):
            place = lax.rem(x + j // ny, nx) * ny + lax.rem(y + j % ny, ny)
            rows = rows_of(core * d_half + place * d_rows, d_rows)
            remote(dpart.at[k, rows], dp.at[k, j - 1], dp_s, dp_r.at[k], plane_peer(j)).start()

    def dz_stage(k):
        landed(dp.at[k], dp_r.at[k])
        total = dpart[k, mine_d, :]
        for j in range(nx * ny - 1):
            total += dp[k, j]
        dz[k, z] = total
        for j in range(1, nz):
            remote(dz.at[k, z], dz.at[k, z], dz_s, dz_r.at[k], z_peer(j)).start()

    def ap_stage(k):
        landed(dz.at[k, pl.ds(0, nz - 1)], dz_r.at[k])
        total = dinv[k]
        for j in range(nz):
            total += dz[k, j]
        full[k, mine_d, :] = total
        place = full.at[k, mine_d]
        for j in range(1, nx * ny):
            remote(place, place, ap_s, ap_r.at[k], plane_peer(j)).start()

    def ac_stage(k):
        landed(dp.at[k], ap_r.at[k])
        place = full.at[k, rows_of(core * d_half, d_half)]
        remote(place, place, ac_s, ac_r.at[k], sibling).start()

    def out_copy(k):
        cols = pl.ds(pl.multiple_of(k * ch, ch), ch)
        return pltpu.make_async_copy(full.at[k], diag_hbm.at[:, cols], out_sem.at[k])

    def out_stage(k):
        landed(dc.at[k], ac_r.at[k])
        out_copy(k).start()

    for k in range(chunks):
        dinv_copy(k).wait()

    stages = {
        "ry": ry_stage, "dot": dot_stage, "dp": dp_stage, "dz": dz_stage, "ap": ap_stage, "ac": ac_stage, "out": out_stage,
    }
    masks = rb * ncol // 32 // 4

    per = max(1, per_way // 4)
    ready = (per_way - 1 + HOP * (nz - 1)) // per + 1

    @pl.loop(0, 4 * chunks + ready + 3 + STAGES["out"])
    def _(u):
        @pl.when(u < 4 * (chunks - 1) + ready)
        def _():
            pl.when(jnp.logical_and(u % 4 == 0, u // 4 + AHEAD < chunks))(lambda: send_source(u // 4 + AHEAD))

            @pl.loop(0, per)
            def _(n):
                gather_step(u * per + n)

        @pl.when(u < 4)
        def _():
            @pl.loop(0, masks)
            def _(n):
                mask_rows(u * masks + n)

        since = u - ready

        @pl.when(jnp.logical_and(since >= 0, since < 4 * chunks))
        def _():
            product(since // 4, since % 4)
            pl.when(since % 4 == 3)(lambda: rc_send(since // 4))

        for name, after in sorted(STAGES.items(), key=lambda item: -item[1]):
            since = u - ready - 3 - after
            runs = jnp.logical_and(since % 4 == 0, jnp.logical_and(since >= 0, since < 4 * chunks))
            pl.when(runs)(lambda name=name, since=since: stages[name](since // 4))

    for k in range(chunks):
        out_copy(k).wait()
    sent(fac_ref, src_sem)
    pl.when(jnp.logical_not(on_diag))(lambda: sent(fac_ref, src_sem))
    pl.when(up < nz - 1)(lambda: sent(gath.at[:, pl.ds(0, per_way)], fwd_sem.at[0]))
    pl.when(down < nz - 1)(lambda: sent(gath.at[:, pl.ds(per_way, per_way)], fwd_sem.at[1]))
    sent(rc, rc_s)
    for ref, sem in ((ry, ry_s), (dc, dc_s), (dp, dp_s), (dz.at[:, pl.ds(0, nz - 1)], dz_s), (dp, ap_s), (dc, ac_s)):
        sent(ref, sem)


def make(g):
    nz, xhn, xln, ny, w, ch, rb = (g[k] for k in ("NZ", "XH", "XL", "NY", "W", "CH", "RB"))
    nx, chunks, ncol = xhn * xln, w // ch, xln * ny * 2
    n = rb * ncol
    dma = pltpu.SemaphoreType.DMA
    d_half, d_rows = w // 2, w // 2 // (nx * ny)

    def body(inverse, pattern, factor, diag_inverse):
        panel, diag = pl.pallas_call(
            functools.partial(kernel, g),
            out_shape=(jax.ShapeDtypeStruct((chunks, rb, ch), F32), jax.ShapeDtypeStruct((w, w), F32)),
            in_specs=[
                pl.BlockSpec(memory_space=pl.ANY),
                pl.BlockSpec(memory_space=pltpu.SMEM),
                pl.BlockSpec(memory_space=pltpu.VMEM),
                pl.BlockSpec(memory_space=pl.ANY),
            ],
            out_specs=(pl.BlockSpec(memory_space=pltpu.VMEM), pl.BlockSpec(memory_space=pl.ANY)),
            scratch_shapes=[
                pltpu.VMEM((n, n), F32),
                pltpu.VMEM((n, n), BF16),
                pltpu.VMEM((n, n), BF16),
                pltpu.VMEM((chunks, ncol, rb, ch), F32),
                pltpu.VMEM((chunks, n, ch), BF16),
                pltpu.VMEM((chunks, n, ch), BF16),
                pltpu.VMEM((chunks, n, ch), F32),
                pltpu.VMEM((chunks, n // 2, ch), F32),
                pltpu.VMEM((chunks, xln * ny - 1, rb, ch), F32),
                pltpu.VMEM((w, rb), BF16),
                pltpu.VMEM((w, rb), BF16),
                pltpu.VMEM((chunks, w, ch), F32),
                pltpu.VMEM((chunks, d_half, ch), F32),
                pltpu.VMEM((chunks, nx * ny - 1, d_rows, ch), F32),
                pltpu.VMEM((chunks, nz, d_rows, ch), F32),
                pltpu.VMEM((chunks, w, ch), F32),
                pltpu.VMEM((chunks, d_rows, ch), F32),
                dma((1 + chunks,)),
                dma((chunks, ncol)),
                dma,
                dma((2,)),
            ]
            + [dma, dma((chunks,))] * 7
            + [dma((chunks,))],
            compiler_params=pltpu.CompilerParams(
                collective_id=0, has_side_effects=True, vmem_limit_bytes=63 * 2**20
            ),
        )(inverse, pattern, factor, diag_inverse)
        return panel.transpose(1, 0, 2).reshape(rb, w), diag

    return body


def solution(mesh):
    return jax.shard_map(
        make(FULL),
        mesh=mesh,
        in_specs=(P("row", "col"), P(), P(("row", "col"), None), P()),
        out_specs=(P(("row", "col"), None), P()),
        check_vma=False,
    )
```

time: 241 us -> 205 us (0.85)
  Pallas kernels: 234 us -> 197 us
    pallas_call x1, Pallas kernels: 234 us -> 197 us  [body(): pl.pallas_call(functools.partial(kernel, g), out_shape=(jax.ShapeDtypeStr...]
where the time goes in v3:
time: 205 us
  Pallas kernels  197 us (96%)
  local copies, waits for them, and re-layouts  6.56 us (3%)
    pallas_call x1, Pallas kernels, body(): pl.pallas_call(functools.partial(kernel, g), out_shape=(jax.ShapeDtypeStr...  197 us
    unnamed x1, local copies, waits for them, and re-layouts  4.79 us

profile of v3, /device:TPU:1, one launch (start us, length us, event | category | flops | bytes accessed | tf_op | source)
XLA Modules:
  0.0 204.6 jit_solution(8229620690417335483)
XLA Ops:
  0.6 197.4 %shard_map.59 = (f32[8,96,128]{2,1,0:T(8,128)}, f32[1024,1024]{1,0:T(8,128)}) custom-call(f32[1536,1536]{1,0:T(8,128)} %inv_hbm.1, s32[48,48]{1,0:T(8,128)} %pat_ref.1, f32[96,1024]{1,0:T(8,128)} %fac_ref.1, f32[1024,1024]{1,0:T(8,128)} %dinv_hbm.1), custom_call_target="tpu_custom_call" | custom-call | tf_op jit(solution)/shard_map/pallas_call | solution.py:289
  198.0 1.8 copy_bitcast_fusion
  199.8 4.8 %copy.10 = f32[1024,1024]{1,0:T(8,128)} copy(f32[1024,1024]{1,0:T(8,128)} %get-tuple-element.9) | data formatting | bytes 8388608

commit v4 on v3

--- a/solution.py
+++ b/solution.py
@@ -12,9 +12,10 @@
 BF16 = jnp.bfloat16
 
 FULL = {"NZ": 8, "XH": 2, "XL": 2, "NY": 4, "W": 1024, "CH": 128, "RB": 96, "B": 512}
-STAGES = {"ry": 1, "dot": 5, "dp": 7, "dz": 10, "ap": 12, "ac": 15, "out": 16}
+STAGES = {"ry": 3, "dot": 9, "da": 12, "db": 17, "dz": 21, "ab": 25, "aa": 29, "ac": 34, "out": 37}
 HOP = 4
-AHEAD = 1
+AHEAD = 2
+LAG = 2
 
 
 def split(value):
@@ -24,9 +25,9 @@
 
 def kernel(
     g, inv_hbm, pat_ref, fac_ref, dinv_hbm, panel_ref, diag_hbm,
-    stage, ih, il, gath, fh, fl, part, rc, ry, fth, ftl, dpart, dc, dp, dz, full, dinv,
-    load_sem, got, src_sem, fwd_sem, rc_s, rc_r, ry_s, ry_r, dc_s, dc_r, dp_s, dp_r,
-    dz_s, dz_r, ap_s, ap_r, ac_s, ac_r, out_sem,
+    stage, ih, il, relayed, gath, fh, fl, part, rc, ry, fth, ftl, dpart, dc, da, db, dz, full, dinv,
+    load_sem, got, relay_got, src_sem, relay_sem, fwd_sem, rc_s, rc_r, ry_s, ry_r, dc_s, dc_r, da_s, da_r, db_s, db_r,
+    dz_s, dz_r, ab_s, ab_r, aa_s, aa_r, ac_s, ac_r, out_sem,
 ):
     nz, xhn, xln, ny, w, ch, rb = (g[k] for k in ("NZ", "XH", "XL", "NY", "W", "CH", "RB"))
     nx, chunks, ncol = xhn * xln, w // ch, xln * ny * 2
@@ -45,6 +46,12 @@
     def plane_peer(j):
         return at(z, lax.rem(x + j // ny, nx), lax.rem(y + j % ny, ny), core)
 
+    def x_peer(j):
+        return at(z, lax.rem(x + j, nx), y, core)
+
+    def y_peer(j):
+        return at(z, x, lax.rem(y + j, ny), core)
+
     def row_peer(j):
         return at(z, xh * xln + lax.rem(xl + j // ny, xln), lax.rem(y + j % ny, ny), core)
 
@@ -54,6 +61,8 @@
     down = lax.rem(nz - up, nz)
     is_root = up == 0
     on_diag = row == col
+    is_relay = jnp.logical_and(y == lax.rem(z, ny), core == xh)
+    own_relay = (row, xl * (2 * ny) + lax.rem(z, ny) * 2 + xh)
 
     def remote(src, dst, send, recv, dev):
         return pltpu.make_async_remote_copy(
@@ -68,12 +77,13 @@
 
     load = pltpu.make_async_copy(inv_hbm, stage, load_sem.at[0])
     load.start()
-    d_half, d_rows = w // 2, w // 2 // (nx * ny)
+    d_half, d_a, d_rows = w // 2, w // 2 // ny, w // 2 // (nx * ny)
 
     def rows_of(first, size):
         return pl.ds(pl.multiple_of(first, size), size)
 
-    mine_d = rows_of(core * d_half + (x * ny + y) * d_rows, d_rows)
+    y_base = core * d_half + y * d_a
+    mine_d = rows_of(y_base + x * d_rows, d_rows)
 
     def dinv_copy(k):
         cols = pl.ds(pl.multiple_of(k * ch, ch), ch)
@@ -93,27 +103,49 @@
     for j in range(1, nx * ny):
         greet(plane_peer(j))
     others = 1 + (nz - 1) + (nx * ny - 1)
-    for a in range(xhn):
-        pl.when(jnp.logical_not(jnp.logical_and(on_diag, xh == a)))(lambda a=a: greet((z * xhn + a, row)))
+    pl.when(jnp.logical_not(is_relay))(lambda: greet(own_relay))
+
+    @pl.when(is_relay)
+    def _():
+        for j in range(2 * ny):
+            other = xl * (2 * ny) + j
+            pl.when(other != col)(lambda other=other: greet((row, other)))
+        for a in range(xhn):
+            pl.when(jnp.logical_not(jnp.logical_and(on_diag, xh == a)))(lambda a=a: greet((z * xhn + a, row)))
 
     @pl.when(is_root)
     def _():
-        @pl.loop(0, ncol)
-        def _(j):
-            pl.when(jnp.logical_not(jnp.logical_and(on_diag, j == col)))(lambda: greet((z * xhn + core, j)))
+        for j in range(xln):
+            other = j * (2 * ny) + y * 2 + core
+            pl.when(jnp.logical_not(jnp.logical_and(on_diag, other == col)))(
+                lambda other=other: greet((z * xhn + core, other))
+            )
 
     mine = jnp.where(on_diag, 1, 0)
-    pl.semaphore_wait(barrier, others + xhn - mine + jnp.where(is_root, ncol - mine, 0))
+    feed = jnp.where(is_relay, 2 * ny - 1 + xhn - mine, 1) + jnp.where(is_root, xln - mine, 0)
+    pl.semaphore_wait(barrier, others + feed)
 
     def send_source(k):
         src = fac_ref.at[:, pl.ds(pl.multiple_of(k * ch, ch), ch)]
-        dst = gath.at[k, col]
-        for a in range(xhn):
-            here = jnp.logical_and(on_diag, xh == a)
-            pl.when(jnp.logical_not(here))(
-                lambda a=a: remote(src, dst, src_sem, got.at[k, col], (z * xhn + a, row)).start()
-            )
-            pl.when(here)(lambda: pltpu.make_async_copy(src, dst, got.at[k, col]).start())
+        dst, arrives = relayed.at[k, y * 2 + core], relay_got.at[k, y * 2 + core]
+        pl.when(jnp.logical_not(is_relay))(lambda: remote(src, dst, src_sem, arrives, own_relay).start())
+        pl.when(is_relay)(lambda: pltpu.make_async_copy(src, dst, arrives).start())
+
+    def relay_step(t):
+        k, i = t // per_way, t % per_way
+        piece, place = relayed.at[k, i], xl * (2 * ny) + i
+
+        @pl.when(is_relay)
+        def _():
+            landed(piece, relay_got.at[k, i])
+            for a in range(xhn):
+                here = jnp.logical_and(on_diag, xh == a)
+                pl.when(jnp.logical_not(here))(
+                    lambda a=a: remote(
+                        piece, gath.at[k, place], relay_sem, got.at[k, place], (z * xhn + a, row)
+                    ).start()
+                )
+                pl.when(here)(lambda: pltpu.make_async_copy(piece, gath.at[k, place], got.at[k, place]).start())
 
     for k in range(min(AHEAD, chunks)):
         send_source(k)
@@ -136,7 +168,7 @@
 
     def gather_step(t):
         for way, far, step in ((0, up, 1), (1, down, nz - 1)):
-            p = t - HOP * far
+            p = t - HOP * far - LAG
 
             @pl.when(jnp.logical_and(p >= 0, p < pieces))
             def _(way=way, far=far, step=step, p=p):
@@ -188,35 +220,50 @@
         dpart[k] = update
         remote(dpart.at[k, rows_of((1 - core) * d_half, d_half)], dc.at[k], dc_s, dc_r.at[k], sibling).start()
 
-    def dp_stage(k):
+    def da_stage(k):
         landed(dc.at[k], dc_r.at[k])
         dpart[k, rows_of(core * d_half, d_half), :] += dc[k]
-        for j in range(1, nx * ny):
-            place = lax.rem(x + j // ny, nx) * ny + lax.rem(y + j % ny, ny)
-            rows = rows_of(core * d_half + place * d_rows, d_rows)
-            remote(dpart.at[k, rows], dp.at[k, j - 1], dp_s, dp_r.at[k], plane_peer(j)).start()
+        for j in range(1, ny):
+            rows = rows_of(core * d_half + lax.rem(y + j, ny) * d_a, d_a)
+            remote(dpart.at[k, rows], da.at[k, j - 1], da_s, da_r.at[k], y_peer(j)).start()
+
+    def db_stage(k):
+        landed(da.at[k], da_r.at[k])
+        total = dpart[k, rows_of(y_base, d_a), :]
+        for j in range(ny - 1):
+            total += da[k, j]
+        dpart[k, rows_of(y_base, d_a), :] = total
+        for j in range(1, nx):
+            rows = rows_of(y_base + lax.rem(x + j, nx) * d_rows, d_rows)
+            remote(dpart.at[k, rows], db.at[k, j - 1], db_s, db_r.at[k], x_peer(j)).start()
 
     def dz_stage(k):
-        landed(dp.at[k], dp_r.at[k])
+        landed(db.at[k], db_r.at[k])
         total = dpart[k, mine_d, :]
-        for j in range(nx * ny - 1):
-            total += dp[k, j]
+        for j in range(nx - 1):
+            total += db[k, j]
         dz[k, z] = total
         for j in range(1, nz):
             remote(dz.at[k, z], dz.at[k, z], dz_s, dz_r.at[k], z_peer(j)).start()
 
-    def ap_stage(k):
+    def ab_stage(k):
         landed(dz.at[k, pl.ds(0, nz - 1)], dz_r.at[k])
         total = dinv[k]
         for j in range(nz):
             total += dz[k, j]
         full[k, mine_d, :] = total
         place = full.at[k, mine_d]
-        for j in range(1, nx * ny):
-            remote(place, place, ap_s, ap_r.at[k], plane_peer(j)).start()
+        for j in range(1, nx):
+            remote(place, place, ab_s, ab_r.at[k], x_peer(j)).start()
+
+    def aa_stage(k):
+        landed(db.at[k], ab_r.at[k])
+        place = full.at[k, rows_of(y_base, d_a)]
+        for j in range(1, ny):
+            remote(place, place, aa_s, aa_r.at[k], y_peer(j)).start()
 
     def ac_stage(k):
-        landed(dp.at[k], ap_r.at[k])
+        landed(da.at[k], aa_r.at[k])
         place = full.at[k, rows_of(core * d_half, d_half)]
         remote(place, place, ac_s, ac_r.at[k], sibling).start()
 
@@ -232,12 +279,13 @@
         dinv_copy(k).wait()
 
     stages = {
-        "ry": ry_stage, "dot": dot_stage, "dp": dp_stage, "dz": dz_stage, "ap": ap_stage, "ac": ac_stage, "out": out_stage,
+        "ry": ry_stage, "dot": dot_stage, "da": da_stage, "db": db_stage, "dz": dz_stage,
+        "ab": ab_stage, "aa": aa_stage, "ac": ac_stage, "out": out_stage,
     }
     masks = rb * ncol // 32 // 4
 
     per = max(1, per_way // 4)
-    ready = (per_way - 1 + HOP * (nz - 1)) // per + 1
+    ready = (per_way - 1 + HOP * (nz - 1) + LAG) // per + 1
 
     @pl.loop(0, 4 * chunks + ready + 3 + STAGES["out"])
     def _(u):
@@ -247,6 +295,7 @@
 
             @pl.loop(0, per)
             def _(n):
+                pl.when(u * per + n < pieces)(lambda: relay_step(u * per + n))
                 gather_step(u * per + n)
 
         @pl.when(u < 4)
@@ -269,13 +318,15 @@
 
     for k in range(chunks):
         out_copy(k).wait()
-    sent(fac_ref, src_sem)
-    pl.when(jnp.logical_not(on_diag))(lambda: sent(fac_ref, src_sem))
+    pl.when(jnp.logical_not(is_relay))(lambda: sent(fac_ref, src_sem))
+    pl.when(is_relay)(lambda: sent(relayed, relay_sem))
+    pl.when(jnp.logical_and(is_relay, jnp.logical_not(on_diag)))(lambda: sent(relayed, relay_sem))
     pl.when(up < nz - 1)(lambda: sent(gath.at[:, pl.ds(0, per_way)], fwd_sem.at[0]))
     pl.when(down < nz - 1)(lambda: sent(gath.at[:, pl.ds(per_way, per_way)], fwd_sem.at[1]))
     sent(rc, rc_s)
-    for ref, sem in ((ry, ry_s), (dc, dc_s), (dp, dp_s), (dz.at[:, pl.ds(0, nz - 1)], dz_s), (dp, ap_s), (dc, ac_s)):
+    for ref, sem in ((ry, ry_s), (dc, dc_s), (da, da_s), (db, db_s), (db, ab_s), (da, aa_s), (dc, ac_s)):
         sent(ref, sem)
+    sent(dz.at[:, pl.ds(0, nz - 1)], dz_s)
 
 
 def make(g):
@@ -283,7 +334,7 @@
     nx, chunks, ncol = xhn * xln, w // ch, xln * ny * 2
     n = rb * ncol
     dma = pltpu.SemaphoreType.DMA
-    d_half, d_rows = w // 2, w // 2 // (nx * ny)
+    d_half, d_a, d_rows = w // 2, w // 2 // ny, w // 2 // (nx * ny)
 
     def body(inverse, pattern, factor, diag_inverse):
         panel, diag = pl.pallas_call(
@@ -300,6 +351,7 @@
                 pltpu.VMEM((n, n), F32),
                 pltpu.VMEM((n, n), BF16),
                 pltpu.VMEM((n, n), BF16),
+                pltpu.VMEM((chunks, 2 * ny, rb, ch), F32),
                 pltpu.VMEM((chunks, ncol, rb, ch), F32),
                 pltpu.VMEM((chunks, n, ch), BF16),
                 pltpu.VMEM((chunks, n, ch), BF16),
@@ -310,16 +362,19 @@
                 pltpu.VMEM((w, rb), BF16),
                 pltpu.VMEM((chunks, w, ch), F32),
                 pltpu.VMEM((chunks, d_half, ch), F32),
-                pltpu.VMEM((chunks, nx * ny - 1, d_rows, ch), F32),
+                pltpu.VMEM((chunks, ny - 1, d_a, ch), F32),
+                pltpu.VMEM((chunks, nx - 1, d_rows, ch), F32),
                 pltpu.VMEM((chunks, nz, d_rows, ch), F32),
                 pltpu.VMEM((chunks, w, ch), F32),
                 pltpu.VMEM((chunks, d_rows, ch), F32),
                 dma((1 + chunks,)),
                 dma((chunks, ncol)),
+                dma((chunks, 2 * ny)),
+                dma,
                 dma,
                 dma((2,)),
             ]
-            + [dma, dma((chunks,))] * 7
+            + [dma, dma((chunks,))] * 9
             + [dma((chunks,))],
             compiler_params=pltpu.CompilerParams(
                 collective_id=0, has_side_effects=True, vmem_limit_bytes=63 * 2**20

time: 205 us -> 191 us (0.932)
  Pallas kernels: 197 us -> 184 us
    pallas_call x1, Pallas kernels: 197 us -> 184 us  [body(): pl.pallas_call(functools.partial(kernel, g), out_shape=(jax.ShapeDtypeStr...]
where the time goes in v4:
time: 191 us
  Pallas kernels  184 us (96%)
  local copies, waits for them, and re-layouts  6.56 us (3%)
    pallas_call x1, Pallas kernels, body(): pl.pallas_call(functools.partial(kernel, g), out_shape=(jax.ShapeDtypeStr...  184 us
    unnamed x1, local copies, waits for them, and re-layouts  4.79 us

profile of v4, /device:TPU:1, one launch (start us, length us, event | category | flops | bytes accessed | tf_op | source)
XLA Modules:
  0.0 191.3 jit_solution(2934002110299687610)
XLA Ops:
  0.6 184.1 %shard_map.59 = (f32[8,96,128]{2,1,0:T(8,128)}, f32[1024,1024]{1,0:T(8,128)}) custom-call(f32[1536,1536]{1,0:T(8,128)} %inv_hbm.1, s32[48,48]{1,0:T(8,128)} %pat_ref.1, f32[96,1024]{1,0:T(8,128)} %fac_ref.1, f32[1024,1024]{1,0:T(8,128)} %dinv_hbm.1), custom_call_target="tpu_custom_call" | custom-call | tf_op jit(solution)/shard_map/pallas_call | solution.py:340
  184.7 1.8 copy_bitcast_fusion
  186.5 4.8 %copy.10 = f32[1024,1024]{1,0:T(8,128)} copy(f32[1024,1024]{1,0:T(8,128)} %get-tuple-element.9) | data formatting | bytes 8388608

commit v5 on v4

--- a/solution.py
+++ b/solution.py
@@ -14,7 +14,7 @@
 FULL = {"NZ": 8, "XH": 2, "XL": 2, "NY": 4, "W": 1024, "CH": 128, "RB": 96, "B": 512}
 STAGES = {"ry": 3, "dot": 9, "da": 12, "db": 17, "dz": 21, "ab": 25, "aa": 29, "ac": 34, "out": 37}
 HOP = 4
-AHEAD = 2
+AHEAD = 1
 LAG = 2
 
 

time: 191 us -> 190 us (level)
  no operation moved by 1% of the time
where the time goes in v5:
time: 190 us
  Pallas kernels  183 us (96%)
  local copies, waits for them, and re-layouts  6.56 us (3%)
    pallas_call x1, Pallas kernels, body(): pl.pallas_call(functools.partial(kernel, g), out_shape=(jax.ShapeDtypeStr...  183 us
    unnamed x1, local copies, waits for them, and re-layouts  4.79 us

profile of v5, /device:TPU:1, one launch (start us, length us, event | category | flops | bytes accessed | tf_op | source)
XLA Modules:
  0.0 189.7 jit_solution(9949234482995899994)
XLA Ops:
  0.6 182.5 %shard_map.59 = (f32[8,96,128]{2,1,0:T(8,128)}, f32[1024,1024]{1,0:T(8,128)}) custom-call(f32[1536,1536]{1,0:T(8,128)} %inv_hbm.1, s32[48,48]{1,0:T(8,128)} %pat_ref.1, f32[96,1024]{1,0:T(8,128)} %fac_ref.1, f32[1024,1024]{1,0:T(8,128)} %dinv_hbm.1), custom_call_target="tpu_custom_call" | custom-call | tf_op jit(solution)/shard_map/pallas_call | solution.py:340
  183.1 1.8 copy_bitcast_fusion
  184.9 4.8 %copy.10 = f32[1024,1024]{1,0:T(8,128)} copy(f32[1024,1024]{1,0:T(8,128)} %get-tuple-element.9) | data formatting | bytes 8388608
